TPU v7x, 128 devices: a whole 4x4x4 slice. The times are simulated.
128 devices in a mesh: row: 16 (over x, y_lo, core), col: 8 (over z, y_hi).
Axes of the slice: x: 4, y: 4 (y_hi: 2, y_lo: 2; y = y_hi * 2 + y_lo), z: 4, core: 2. Of those that a mesh axis runs over, the one named last changes fastest.
Arguments:
- amplitudes: bfloat16 [24576, 24576], P('col', 'row'), may hold values from -0.0390625 to 0.0390625
- cholesky: bfloat16 [24576, 1280], P(('row', 'col')), may hold values from -5 to 5
- occ_map: int32 [24576], replicated, may hold values from 0 to 47
- vir_map: int32 [24576], replicated, may hold values from 0 to 511
Outputs:
- new_amplitudes: bfloat16 [24576, 24576], P('col', 'row')
All inputs are finite; a program needn't handle non-finite values.
Results may differ from a plain program's by a relative error of at most 0.0056.
Values may be sent and summed in bfloat16 or wider, within the bound.
A program may use at most 128 MiB of HBM per device.

v0:
```python
import jax
import jax.numpy as jnp
from jax import lax
from jax.sharding import PartitionSpec as P

NOCC = 48
NVIR = 512


def broadcast(x, axis, root):
    mine = lax.axis_index(axis) == root
    return lax.psum(jnp.where(mine, x, jnp.zeros_like(x)), axis)


def pair_gap(occ_map, vir_map):
    occ = occ_map.astype(jnp.float32)
    vir = vir_map.astype(jnp.float32)
    return 0.5 + 2.5 * jnp.sqrt(vir / NVIR) + (0.5 + 2.5 * occ / NOCC)


def body(amplitudes, cholesky, occ_map, vir_map):
    tile_rows, tile_cols = amplitudes.shape
    row_index = lax.axis_index("row")
    col_index = lax.axis_index("col")
    q_start = row_index * tile_cols
    p_start = col_index * tile_rows
    offset = q_start - p_start
    on_diag = jnp.logical_and(offset >= 0, offset < tile_rows).astype(jnp.float32)
    safe_offset = jnp.clip(offset, 0, tile_rows - tile_cols)
    piece = lax.all_gather(cholesky, "col", axis=0, tiled=True)
    count = piece.shape[0]
    total = jnp.dot(amplitudes, piece, preferred_element_type=jnp.float32)
    current = lax.dynamic_slice_in_dim(total, safe_offset, count, 0)
    partial_value = lax.dynamic_update_slice_in_dim(
        total, current + on_diag * piece.astype(jnp.float32), safe_offset, 0
    )
    y_block = lax.psum(partial_value, "row").astype(jnp.bfloat16)
    q_root = q_start // tile_rows
    q_inside = q_start % tile_rows
    own_part = lax.dynamic_slice_in_dim(y_block, q_inside, tile_cols, 0)
    y_cols = broadcast(own_part, "col", q_root)
    cycle = lax.dot_general(
        y_block, y_cols, (((1,), (1,)), ((), ())), preferred_element_type=jnp.float32
    )
    gap_rows = pair_gap(
        lax.dynamic_slice_in_dim(occ_map, p_start, tile_rows, 0),
        lax.dynamic_slice_in_dim(vir_map, p_start, tile_rows, 0),
    )
    gap_cols = pair_gap(
        lax.dynamic_slice_in_dim(occ_map, q_start, tile_cols, 0),
        lax.dynamic_slice_in_dim(vir_map, q_start, tile_cols, 0),
    )
    return (-cycle / (gap_rows[:, None] + gap_cols[None, :])).astype(jnp.bfloat16)


def solution(mesh):
    return jax.shard_map(
        body,
        mesh=mesh,
        in_specs=(P("col", "row"), P(("row", "col"), None), P(), P()),
        out_specs=P("col", "row"),
        check_vma=False,
    )
```

profile of v0, /device:TPU:1, one launch (start us, length us, event | category | flops | bytes accessed | tf_op | source)
XLA Modules:
  0.0 667.7 jit_solution(5515515563496372518)
XLA Ops:
  6.5 0.0 all-gather.2.cloned.1.call-start
  6.5 0.7 all-gather.2.cloned.1.call-update
  7.3 0.0 all-reduce.3.cloned.1.call-start
  7.4 74.6 %all-gather.2.cloned.1.call-done = bf16[1536,1280]{1,0:T(8,128)(2,1)} async-done(((bf16[192,1280]{1,0:T(8,128)(2,1)}), bf16[1536,1280]{1,0:T(8,128)(2,1)}) %all-gather.2.cloned.1.call-update) | async-done | bytes 3932176 | tf_op jit(solution)/shard_map/all_gather | solution.py:30
  81.9 16.7 %fusion = f32[3072,1280]{1,0:T(8,128)S(1)} fusion(bf16[3072,1536]{1,0:T(8,128)(2,1)} %param.4, bf16[1536,1280]{1,0:T(8,128)(2,1)} %all-gather.2.cloned.1.call-done), kind=kOutput, calls=%fused_computation.5 | convolution fusion | flops 12079595520 | bytes 29097984 | tf_op jit(solution)/shard_map/dot_general | solution.py:32
  98.6 0.0 copy-start
  98.6 5.5 copy-done
  104.1 6.7 %multiply_add_fusion = f32[1536,1280]{1,0:T(8,128)} fusion(bf16[1536,1280]{1,0:T(8,128)(2,1)} %all-gather.2.cloned.1.call-done, f32[3072,1280]{1,0:T(8,128)S(1)} %fusion, s32[]{:T(128)S(6)} %min.4, f32[]{:T(128)S(6)} %convert_element_type.24), kind=kLoop, calls=%fused_computation.1 | loop fusion | flops 5898240 | bytes 19660808 | tf_op jit(solution)/shard_map/add | solution.py:35
  110.9 19.0 %dynamic_update_slice.3 = f32[3072,1280]{1,0:T(8,128)} dynamic-update-slice(f32[3072,1280]{1,0:T(8,128)} %copy-done, f32[1536,1280]{1,0:T(8,128)} %multiply_add_fusion, s32[]{:T(128)S(6)} %min.4, s32[]{:T(128)} %constant.40.clone.1) | dynamic-update-slice | bytes 15728644 | tf_op jit(solution)/shard_map/dynamic_update_slice | solution.py:34
  129.8 334.6 %all-reduce.4 = bf16[3072,1280]{1,0:T(8,128)(2,1)} all-reduce(f32[3072,1280]{1,0:T(8,128)} %dynamic_update_slice.3), channel_id=1, replica_groups=mesh['row'=16,'col'=8] {'row'}, use_global_device_ids=true, to_apply=%region_0.1 | all-reduce | flops 3932160 | bytes 23592960 | tf_op jit(solution)/shard_map/psum | solution.py:37
  464.5 5.2 dynamic-slice_select_fusion
  469.7 0.0 all-reduce.3.cloned.1.call-update
  469.7 0.8 add_add_fusion.1
  470.5 0.7 add_add_fusion
  471.3 170.8 %all-reduce.3.cloned.1.call-done = bf16[1536,1280]{1,0:T(8,128)(2,1)} async-done(((bf16[1536,1280]{1,0:T(8,128)(2,1)}), bf16[1536,1280]{1,0:T(8,128)(2,1)}) %all-reduce.3.cloned.1.call-update) | async-done | bytes 3932176 | tf_op jit(solution)/shard_map/psum | solution.py:12
  642.1 18.7 %divide_convert_fusion = bf16[3072,1536]{1,0:T(8,128)(2,1)} fusion(bf16[3072,1280]{1,0:T(8,128)(2,1)} %all-reduce.4, bf16[1536,1280]{1,0:T(8,128)(2,1)} %all-reduce.3.cloned.1.call-done, f32[1536]{0:T(1024)S(1)} %add_add_fusion.1, f32[3072]{0:T(1024)S(1)} %add_add_fusion), kind=kOutput, calls=%fused_computation | convolution fusion | flops 12098469888 | bytes 21252096 | tf_op jit(solution)/shard_map/dot_general | solution.py:42
Async XLA Ops:
  6.5 75.4 %all-gather.2.cloned.1.call-start = ((), (), s32[]{:S(2)}) async-start(), calls=%async_computation | async-start | bytes 4423680 | tf_op jit(solution)/shard_map/all_gather | solution.py:30
  7.3 634.9 %all-reduce.3.cloned.1.call-start = ((), (), s32[]{:S(2)}) async-start(), calls=%async_computation.1 | async-start | bytes 7864320 | tf_op jit(solution)/shard_map/psum | solution.py:12
  98.6 5.5 copy-start
Sparse Core Ops, SparseCore 0:
  9.7 72.2 all-gather.1
  469.8 172.2 all-reduce.2
where the time goes:
time: 668 us
  blocking collectives  335 us (50%)
  waiting for transfers between devices  246 us (37%)
  matrix products  35.4 us (5%)
  local copies, waits for them, and re-layouts  24.5 us (4%)
  other arithmetic  13.5 us (2%)
  between operations  13.5 us (2%)
    psum x1, blocking collectives, body(): y_block = lax.psum(partial_value, 'row').astype(jnp.bfloat16)  335 us
    psum x1, waiting for transfers between devices, broadcast(): return lax.psum(jnp.where(mine, x, jnp.zeros_like(x)), axis)  171 us
    all_gather x1, waiting for transfers between devices, body(): piece = lax.all_gather(cholesky, 'col', axis=0, tiled=True)  74.6 us
    dynamic_update_slice x1, local copies, waits for them, and re-layouts, body(): lax.dynamic_update_slice_in_dim(total, current + on_diag * piece.astype(j...  19 us
    dot_general x1, matrix products, body(): lax.dot_general(y_block, y_cols, (((1,), (1,)), ((), ())), preferred_elem...  18.7 us
    dot_general x1, matrix products, body(): total = jnp.dot(amplitudes, piece, preferred_element_type=jnp.float32)  16.7 us
  transfers between devices with their start and end apart: 2, of which 2 were waited for; matrix products, arithmetic and copies ran while one was open for 0% of the time, Pallas kernels for 0%

commit v1 on v0

v1 whole, which is shorter than its diff:
```python
import jax
import jax.numpy as jnp
from jax import lax
from jax.experimental import pallas as pl
from jax.experimental.pallas import tpu as pltpu
from jax.sharding import PartitionSpec as P

NOCC = 48
NVIR = 512
MESH = pl.DeviceIdType.MESH
BF16 = jnp.bfloat16
F32 = jnp.float32

CHUNKS = 5
ORDER = [
    ("a1", 0), ("a1", 1), ("a1", 2), ("ob1", 0), ("a1", 3), ("a1", 4), ("a2", 0), ("a2", 1),
    ("a2", 2), ("a3", 0), ("a3", 1), ("a3", 2), ("ob2", 0), ("m1", 0), ("m2", 0), ("m1", 1),
    ("b1", 0), ("m2", 1), ("b1", 1), ("m1", 2), ("m2", 2), ("b2", 0), ("b1", 2), ("a2", 3),
    ("b2", 1), ("a2", 4), ("b3", 0), ("a3", 3), ("b2", 2), ("fin", 0), ("a3", 4), ("b3", 1),
    ("m1", 3), ("m2", 3), ("t2", 0), ("b1", 3), ("fin", 1), ("b3", 2), ("m1", 4), ("m2", 4),
    ("d1", 0), ("t2", 1), ("b1", 4), ("b2", 3), ("fin", 2), ("d2", 0), ("b2", 4), ("d1", 1),
    ("t2", 2), ("c2", 0), ("c2", 1), ("c2", 2), ("b3", 3), ("d2", 1), ("d3", 0), ("b3", 4),
    ("fin", 3), ("d1", 2), ("d3", 1), ("fin", 4), ("c3", 0), ("t2", 3), ("c2", 3), ("d2", 2),
    ("t2", 4), ("c3", 1), ("c2", 4), ("c3", 2), ("d3", 2), ("c4", 0), ("d1", 3), ("w", 0),
    ("d2", 3), ("c3", 3), ("d1", 4), ("c4", 1), ("d2", 4), ("w", 1), ("d3", 3), ("c3", 4),
    ("c4", 2), ("d3", 4), ("w", 2), ("c4", 3), ("w", 3), ("c4", 4), ("w", 4),
]

COPIES = [
    "a1", "a2p", "a2m", "a3p", "a3m", "dd", "b1p", "b1m", "b2p", "b2m", "b3",
    "c1", "c2p", "c2m", "c3p", "c3m", "c4", "t1", "t2", "d1", "d2p", "d2m", "d3p", "d3m",
]


def pair_gap(occ_map, vir_map):
    occ = occ_map.astype(jnp.float32)
    vir = vir_map.astype(jnp.float32)
    return 0.5 + 2.5 * jnp.sqrt(vir / NVIR) + (0.5 + 2.5 * occ / NOCC)


def place(x, yl, k, z, yh):
    return x * 4 + yl * 2 + k, z * 2 + yh


def kernel(t_hbm, b_own, rows_out, cols_out, t_v, bg, p_send, p_own, sib, b1s, b1r, b2s, b2r,
           b3s, b3r, rows, cols, t1r, ob1r, ob2r, send_sem, recv_sem, local_sem):
    r, c = lax.axis_index("row"), lax.axis_index("col")
    x, yl, k = r // 4, (r // 2) % 2, r % 2
    z, yh = c // 2, c % 2
    n = CHUNKS
    s = b_own.shape[0]
    w = b_own.shape[1] // n
    half = 8 * s

    xp, xm = place((x + 1) % 4, yl, k, z, yh), place((x + 3) % 4, yl, k, z, yh)
    zp, zm = place(x, yl, k, (z + 1) % 4, yh), place(x, yl, k, (z + 3) % 4, yh)
    low, high = place(x, 1 - yl, k, z, yh), place(x, yl, k, z, 1 - yh)
    other = place(x, yl, 1 - k, z, yh)
    out_z, in_z = place(x, yl, k, (z + x) % 4, yh), place(x, yl, k, (z + 4 - x) % 4, yh)
    mirror_x = (z + 4 - x) % 4
    mirror = place(mirror_x, yh, k, z, yl)
    moves = x != 0
    mirrored = jnp.logical_or(mirror_x != x, yh != yl)

    barrier = pltpu.get_barrier_semaphore()
    for device in (xp, xm, zp, zm, low, high, other):
        pl.semaphore_signal(barrier, inc=1, device_id=device, device_id_type=MESH)

    @pl.when(moves)
    def _():
        for device in (out_z, in_z):
            pl.semaphore_signal(barrier, inc=1, device_id=device, device_id_type=MESH)

    @pl.when(mirrored)
    def _():
        pl.semaphore_signal(barrier, inc=1, device_id=mirror, device_id_type=MESH)

    t_copy = pltpu.make_async_copy(t_hbm, t_v, local_sem.at[2 * n])
    t_copy.start()

    pl.semaphore_wait(barrier, 7 + 2 * moves.astype(jnp.int32) + mirrored.astype(jnp.int32))

    def copy(name, j, src, dst, device):
        at = j * len(COPIES) + COPIES.index(name) if name in COPIES else n * len(COPIES) + j
        return pltpu.make_async_remote_copy(
            src_ref=src, dst_ref=dst, send_sem=send_sem.at[at], recv_sem=recv_sem.at[at],
            device_id=device, device_id_type=MESH,
        )

    def rows_of(block, count):
        return pl.ds(pl.multiple_of(block * s, s), count * s)

    def here(pos):
        return (pos + z) % 4

    sent = []
    waiting = {}

    def send(name, j, src, dst, device, when=None):
        one = copy(name, j, src, dst, device)
        if when is None:
            one.start()
        else:
            pl.when(when)(one.start)
        sent.append((one, when))
        waiting[name, j] = (one, when)

    def arrive(name, j):
        one, when = waiting.pop((name, j))
        if when is None:
            one.wait_recv()
        else:
            pl.when(when)(one.wait_recv)

    def pair_out(name, j, buf, at, p, plus, minus):
        view = buf.at[j, rows_of(at + 2 * p, 2)]
        send(name + "p", j, view, view, plus)
        send(name + "m", j, view, view, minus)

    def pass_on(name, j, buf, at, before, after, q, plus, minus):
        up = buf.at[j, rows_of(at + 2 * before + q, 1)]
        down = buf.at[j, rows_of(at + 2 * after + 1 - q, 1)]
        send(name + "p", j, up, up, plus)
        send(name + "m", j, down, down, minus)

    tile = 2 * s

    def dressed_part(j, start, store):
        def step(i, carry):
            t = t_v[pl.ds(pl.multiple_of(start + i * tile, tile), tile), :]
            store(i, jnp.dot(t, bg[j], preferred_element_type=F32))
            return carry
        lax.fori_loop(0, half // tile, step, 0)

    def partial(j, block, count):
        at = rows_of(block, count)
        return p_own[j % p_own.shape[0], at] + sib[j, at].astype(F32)

    done = {}

    def run(name, j):
        own_a = rows_of(2 * z + yh, 1)
        own_c = rows_of(8 * k + 2 * here(x) + yl, 1)
        if name == "ob1":
            send("ob1", 0, b_own, ob1r, mirror, mirrored)

            @pl.when(jnp.logical_not(mirrored))
            def _():
                ob1r[...] = b_own[...]
        elif name == "ob2":
            arrive("ob1", 0)
            send("ob2", 1, ob1r, ob2r, in_z, moves)

            @pl.when(jnp.logical_not(moves))
            def _():
                ob2r[...] = ob1r[...]
        elif name == "a1":
            bg[j, own_a] = b_own[:, j * w:(j + 1) * w]
            send("a1", j, b_own.at[:, pl.ds(j * w, w)], bg.at[j, own_a], high)
        elif name == "a2":
            arrive("a1", j)
            pair_out("a2", j, bg, 0, z, zp, zm)
        elif name == "a3":
            arrive("a2p", j)
            arrive("a2m", j)
            pass_on("a3", j, bg, 0, (z + 3) % 4, (z + 1) % 4, yh, zp, zm)
        elif name == "m1":
            arrive("a3p", j)
            arrive("a3m", j)
            if not done:
                t_copy.wait()
                done["t"] = True

            def store(i, value):
                p_send[j, pl.ds(pl.multiple_of(i * tile, tile), tile)] = value.astype(BF16)
            dressed_part(j, (1 - k) * half, store)
            send("dd", j, p_send.at[j], sib.at[j], other)
        elif name == "m2":
            def store(i, value):
                p_own[j % p_own.shape[0], pl.ds(pl.multiple_of(i * tile, tile), tile)] = value
            dressed_part(j, k * half, store)
        elif name == "b1":
            arrive("dd", j)
            far = here(x + 2)
            b1s[j, 0] = partial(j, 2 * far + yl, 1).astype(BF16)
            b1s[j, 1] = partial(j, 2 * far + 1 - yl, 1).astype(BF16)
            send("b1p", j, b1s.at[j, 0], b1r.at[j, 0], xp)
            send("b1m", j, b1s.at[j, 1], b1r.at[j, 1], xm)
        elif name == "b2":
            arrive("b1p", j)
            arrive("b1m", j)
            for side, (step, q) in enumerate(((1, yl), (3, 1 - yl))):
                to = here(x + step)
                b2s[j, side, rows_of(q, 1)] = (
                    partial(j, 2 * to + q, 1) + b1r[j, side].astype(F32)).astype(BF16)
                b2s[j, side, rows_of(1 - q, 1)] = partial(j, 2 * to + 1 - q, 1).astype(BF16)
            send("b2p", j, b2s.at[j, 0], b2r.at[j, 0], xp)
            send("b2m", j, b2s.at[j, 1], b2r.at[j, 1], xm)
        elif name == "b3":
            arrive("b2p", j)
            arrive("b2m", j)

            def total(q):
                at = rows_of(q, 1)
                return partial(j, 2 * here(x) + q, 1) + (
                    b2r[j, 0, at].astype(F32) + b2r[j, 1, at].astype(F32))
            b3s[j] = total(1 - yl).astype(BF16)
            send("b3", j, b3s.at[j], b3r.at[j], low)
            p_own[j % p_own.shape[0], rows_of(2 * here(x) + yl, 1)] = total(yl)
        elif name == "fin":
            if "b" not in done:
                arrive("ob2", 1)
                done["b"] = True
            arrive("b3", j)
            value = (p_own[j % p_own.shape[0], rows_of(2 * here(x) + yl, 1)] + b3r[j].astype(F32)
                     + ob2r[:, j * w:(j + 1) * w].astype(F32)).astype(BF16)
            rows[j, own_c] = value
            send("t1", j, rows.at[j, own_c], t1r.at[j], out_z, moves)
            send("c1", j, rows.at[j, own_c], rows.at[j, own_c], low)

            @pl.when(jnp.logical_not(moves))
            def _():
                t1r[j] = value
        elif name == "c2":
            arrive("c1", j)
            pair_out("c2", j, rows, 8 * k, here(x), xp, xm)
        elif name == "c3":
            arrive("c2p", j)
            arrive("c2m", j)
            pass_on("c3", j, rows, 8 * k, here(x + 3), here(x + 1), yl, xp, xm)
        elif name == "c4":
            arrive("c3p", j)
            arrive("c3m", j)
            mine = rows.at[j, rows_of(8 * k, 8)]
            send("c4", j, mine, mine, other)
        elif name == "t2":
            arrive("t1", j)
            at = rows_of(2 * z + yl, 1)
            send("t2", j, t1r.at[j], cols.at[j, at], mirror, mirrored)

            @pl.when(jnp.logical_not(mirrored))
            def _():
                cols[j, at] = t1r[j]
        elif name == "d1":
            arrive("t2", j)
            send("d1", j, cols.at[j, own_a], cols.at[j, own_a], high)
        elif name == "d2":
            arrive("d1", j)
            pair_out("d2", j, cols, 0, z, zp, zm)
        elif name == "d3":
            arrive("d2p", j)
            arrive("d2m", j)
            pass_on("d3", j, cols, 0, (z + 3) % 4, (z + 1) % 4, yh, zp, zm)
        elif name == "w":
            arrive("d3p", j)
            arrive("d3m", j)
            arrive("c4", j)
            at = pl.ds(j * w, w)
            pltpu.make_async_copy(rows.at[j], rows_out.at[:, at], local_sem.at[j]).start()
            pltpu.make_async_copy(cols.at[j], cols_out.at[:, at], local_sem.at[n + j]).start()

    for name, j in ORDER:
        run(name, j)
    for j in range(n):
        at = pl.ds(j * w, w)
        pltpu.make_async_copy(rows.at[j], rows_out.at[:, at], local_sem.at[j]).wait()
        pltpu.make_async_copy(cols.at[j], cols_out.at[:, at], local_sem.at[n + j]).wait()
    for one, when in sent:
        if when is None:
            one.wait_send()
        else:
            pl.when(when)(one.wait_send)


def gather_dressed(amplitudes, cholesky):
    height, width = amplitudes.shape
    s, naux = cholesky.shape
    n = CHUNKS
    w = naux // n
    half = 8 * s
    many = n * len(COPIES) + 2
    return pl.pallas_call(
        kernel,
        out_shape=(
            jax.ShapeDtypeStruct((height, naux), BF16),
            jax.ShapeDtypeStruct((width, naux), BF16),
        ),
        in_specs=[pl.BlockSpec(memory_space=pl.ANY), pl.BlockSpec(memory_space=pltpu.VMEM)],
        out_specs=(pl.BlockSpec(memory_space=pl.ANY), pl.BlockSpec(memory_space=pl.ANY)),
        scratch_shapes=[
            pltpu.VMEM((height, width), BF16),
            pltpu.VMEM((n, 8 * s, w), BF16),
            pltpu.VMEM((n, half, w), BF16),
            pltpu.VMEM((n, half, w), F32),
            pltpu.VMEM((n, half, w), BF16),
            pltpu.VMEM((n, 2, s, w), BF16),
            pltpu.VMEM((n, 2, s, w), BF16),
            pltpu.VMEM((n, 2, 2 * s, w), BF16),
            pltpu.VMEM((n, 2, 2 * s, w), BF16),
            pltpu.VMEM((n, s, w), BF16),
            pltpu.VMEM((n, s, w), BF16),
            pltpu.VMEM((n, 2 * half, w), BF16),
            pltpu.VMEM((n, 8 * s, w), BF16),
            pltpu.VMEM((n, s, w), BF16),
            pltpu.VMEM((s, naux), BF16),
            pltpu.VMEM((s, naux), BF16),
            pltpu.SemaphoreType.DMA((many,)),
            pltpu.SemaphoreType.DMA((many,)),
            pltpu.SemaphoreType.DMA((2 * n + 1,)),
        ],
        compiler_params=pltpu.CompilerParams(
            collective_id=0, has_side_effects=True, vmem_limit_bytes=62 * 2**20),
        cost_estimate=pl.CostEstimate(
            flops=2 * height * width * naux, bytes_accessed=2 * height * width, transcendentals=0),
    )(amplitudes, cholesky)


def body(amplitudes, cholesky, occ_map, vir_map):
    height, width = amplitudes.shape
    p_start = lax.axis_index("col") * height
    q_start = lax.axis_index("row") * width
    rows, cols = gather_dressed(amplitudes, cholesky)
    cycle = lax.dot_general(
        rows, cols, (((1,), (1,)), ((), ())), preferred_element_type=jnp.float32
    )
    gap_rows = pair_gap(
        lax.dynamic_slice_in_dim(occ_map, p_start, height, 0),
        lax.dynamic_slice_in_dim(vir_map, p_start, height, 0),
    )
    gap_cols = pair_gap(
        lax.dynamic_slice_in_dim(occ_map, q_start, width, 0),
        lax.dynamic_slice_in_dim(vir_map, q_start, width, 0),
    )
    return (-cycle / (gap_rows[:, None] + gap_cols[None, :])).astype(jnp.bfloat16)


def solution(mesh):
    return jax.shard_map(
        body,
        mesh=mesh,
        in_specs=(P("col", "row"), P(("row", "col"), None), P(), P()),
        out_specs=P("col", "row"),
        check_vma=False,
    )
```

time: 668 us -> 156 us (0.23)
  blocking collectives: 335 us -> 0 us
  waiting for transfers between devices: 246 us -> 0 us
  Pallas kernels: 0 us -> 133 us
  local copies, waits for them, and re-layouts: 24.5 us -> 0 us
  matrix products: 35.4 us -> 18.7 us
  between operations: 13.5 us -> 0.01 us
  other arithmetic: 13.5 us -> 1.55 us
    psum x1 -> x0, blocking collectives: 335 us -> none  [body(): y_block = lax.psum(partial_value, 'row').astype(jnp.bfloat16)]
    psum x1 -> x0, waiting for transfers between devices: 171 us -> none  [broadcast(): return lax.psum(jnp.where(mine, x, jnp.zeros_like(x)), axis)]
    pallas_call x0 -> x1, Pallas kernels: none -> 133 us  [gather_dressed(): pl.pallas_call(kernel, out_shape=(jax.ShapeDtypeStruct((height, naux), BF...]
    all_gather x1 -> x0, waiting for transfers between devices: 74.6 us -> none  [body(): piece = lax.all_gather(cholesky, 'col', axis=0, tiled=True)]
    dynamic_update_slice x1 -> x0, local copies, waits for them, and re-layouts: 19 us -> none  [body(): lax.dynamic_update_slice_in_dim(total, current + on_diag * piece.astype(j...]
    dot_general x2 -> x1, matrix products: 35.4 us -> 18.7 us  [body(): lax.dot_general(rows, cols, (((1,), (1,)), ((), ())), preferred_element_t...]
    add x1 -> x0, other arithmetic: 6.72 us -> none  [body(): current + on_diag * piece.astype(jnp.float32)]
  transfers between devices with their start and end apart: 2 -> 0, of which waited for: 2 -> 0; matrix products, arithmetic and copies ran while one was open for 0% -> 0% of each run, Pallas kernels for 0% -> 0%
where the time goes in v1:
time: 156 us; the launch traced here: 153 us
  Pallas kernels  133 us (85%)
  matrix products  18.7 us (12%)
    pallas_call x1, Pallas kernels, gather_dressed(): pl.pallas_call(kernel, out_shape=(jax.ShapeDtypeStruct((height, naux), BF...  133 us
    dot_general x1, matrix products, body(): lax.dot_general(rows, cols, (((1,), (1,)), ((), ())), preferred_element_t...  18.7 us

profile of v1, /device:TPU:1, one launch (start us, length us, event | category | flops | bytes accessed | tf_op | source)
XLA Modules:
  0.0 153.3 jit_solution(5441496095300210981)
XLA Ops:
  0.0 0.8 add_add_fusion.1
  0.8 0.7 add_add_fusion
  1.6 133.0 %shard_map.46 = (bf16[3072,1280]{1,0:T(8,128)(2,1)}, bf16[1536,1280]{1,0:T(8,128)(2,1)}) custom-call(bf16[3072,1536]{1,0:T(8,128)(2,1)} %t_hbm.1, bf16[192,1280]{1,0:T(8,128)(2,1)} %b_own.1), custom_call_target="tpu_custom_call" | custom-call | flops 12079595520 | bytes 9437184 | tf_op jit(solution)/shard_map/pallas_call | solution.py:282
  134.6 18.7 %divide_convert_fusion = bf16[3072,1536]{1,0:T(8,128)(2,1)} fusion(bf16[3072,1280]{1,0:T(8,128)(2,1)} %get-tuple-element.7, bf16[1536,1280]{1,0:T(8,128)(2,1)} %get-tuple-element.8, f32[1536]{0:T(1024)S(1)} %add_add_fusion.1, f32[3072]{0:T(1024)S(1)} %add_add_fusion), kind=kOutput, calls=%fused_computation | convolution fusion | flops 12098469888 | bytes 21252096 | tf_op jit(solution)/shard_map/dot_general | solution.py:323

commit v2 on v1

v2 whole, which is shorter than its diff:
```python
import jax
import jax.numpy as jnp
from jax import lax
from jax.experimental import pallas as pl
from jax.experimental.pallas import tpu as pltpu
from jax.sharding import PartitionSpec as P

NOCC = 48
NVIR = 512
MESH = pl.DeviceIdType.MESH
BF16 = jnp.bfloat16
F32 = jnp.float32

WIDTHS = [256, 256, 256, 256, 256]
OWN_SLOTS = 3
SEND_SLOTS = 2
GPARTS = 3
GTILE = 256
ORDER = [
    ("a1", 0), ("a1", 1), ("gap", 0), ("a1", 2), ("ob1", 0), ("a1", 3), ("a1", 4), ("a2", 0),
    ("a2", 1), ("a2", 2), ("a3", 0), ("a3", 1), ("a3", 2), ("ob2", 0), ("m1", 0), ("m2", 0),
    ("m1", 1), ("b1", 0), ("m1", 2), ("m2", 1), ("b1", 1), ("m2", 2), ("b2", 0), ("b1", 2),
    ("a2", 3), ("a2", 4), ("b2", 1), ("b3", 0), ("a3", 3), ("b2", 2), ("fin", 0), ("a3", 4),
    ("b3", 1), ("m1", 3), ("m2", 3), ("t2", 0), ("b1", 3), ("fin", 1), ("b3", 2), ("m1", 4),
    ("m2", 4), ("d1", 0), ("t2", 1), ("b1", 4), ("b2", 3), ("fin", 2), ("d2", 0), ("b2", 4),
    ("d1", 1), ("t2", 2), ("c2", 0), ("c2", 1), ("c2", 2), ("b3", 3), ("d2", 1), ("d3", 0),
    ("b3", 4), ("fin", 3), ("d1", 2), ("d3", 1), ("fin", 4), ("c3", 0), ("t2", 3), ("c2", 3),
    ("d2", 2), ("t2", 4), ("c3", 1), ("c2", 4), ("c3", 2), ("d3", 2), ("c4", 0), ("d1", 3),
    ("w", 0), ("g2", 0), ("g1", 0), ("g0", 0), ("d2", 3), ("c3", 3), ("d1", 4), ("c4", 1),
    ("d2", 4), ("w", 1), ("g2", 1), ("d3", 3), ("g1", 1), ("g0", 1), ("c3", 4), ("c4", 2),
    ("d3", 4), ("w", 2), ("g2", 2), ("c4", 3), ("g1", 2), ("c4", 4), ("g0", 2), ("w", 3),
    ("g2", 3), ("g1", 3), ("g0", 3), ("w", 4), ("g2", 4), ("g1", 4), ("g0", 4),
]

COPIES = [
    "a1", "a2p", "a2m", "a3p", "a3m", "dd", "b1p", "b1m", "b2p", "b2m", "b3",
    "c1", "c2p", "c2m", "c3p", "c3m", "c4", "t1", "t2", "d1", "d2p", "d2m", "d3p", "d3m",
]


def place(x, yl, k, z, yh):
    return x * 4 + yl * 2 + k, z * 2 + yh


def kernel(t_hbm, b_own, occ, vir, out, bg, p_send, p_own, sib, b1r, b2r, b3r, rows, cols, t1r,
           ob1r, ob2r, acc, gap, gap_rows, send_sem, recv_sem, local_sem):
    r, c = lax.axis_index("row"), lax.axis_index("col")
    x, yl, k = r // 4, (r // 2) % 2, r % 2
    z, yh = c // 2, c % 2
    n = len(WIDTHS)
    begin = [sum(WIDTHS[:j]) for j in range(n)]
    s = b_own.shape[0]
    half = 8 * s

    xp, xm = place((x + 1) % 4, yl, k, z, yh), place((x + 3) % 4, yl, k, z, yh)
    zp, zm = place(x, yl, k, (z + 1) % 4, yh), place(x, yl, k, (z + 3) % 4, yh)
    low, high = place(x, 1 - yl, k, z, yh), place(x, yl, k, z, 1 - yh)
    other = place(x, yl, 1 - k, z, yh)
    out_z, in_z = place(x, yl, k, (z + x) % 4, yh), place(x, yl, k, (z + 4 - x) % 4, yh)
    mirror_x = (z + 4 - x) % 4
    mirror = place(mirror_x, yh, k, z, yl)
    moves = x != 0
    mirrored = jnp.logical_or(mirror_x != x, yh != yl)

    barrier = pltpu.get_barrier_semaphore()
    for device in (xp, xm, zp, zm, low, high, other):
        pl.semaphore_signal(barrier, inc=1, device_id=device, device_id_type=MESH)

    @pl.when(moves)
    def _():
        for device in (out_z, in_z):
            pl.semaphore_signal(barrier, inc=1, device_id=device, device_id_type=MESH)

    @pl.when(mirrored)
    def _():
        pl.semaphore_signal(barrier, inc=1, device_id=mirror, device_id_type=MESH)

    t_copy = pltpu.make_async_copy(t_hbm, out, local_sem.at[0])
    t_copy.start()

    pl.semaphore_wait(barrier, 7 + 2 * moves.astype(jnp.int32) + mirrored.astype(jnp.int32))

    def copy(name, j, src, dst, device):
        at = j * len(COPIES) + COPIES.index(name) if name in COPIES else n * len(COPIES) + j
        return pltpu.make_async_remote_copy(
            src_ref=src, dst_ref=dst, send_sem=send_sem.at[at], recv_sem=recv_sem.at[at],
            device_id=device, device_id_type=MESH,
        )

    def rows_of(block, count):
        return pl.ds(pl.multiple_of(block * s, s), count * s)

    def here(pos):
        return (pos + z) % 4

    sent = {}
    waiting = {}

    def send(name, j, src, dst, device, when=None):
        one = copy(name, j, src, dst, device)
        if when is None:
            one.start()
        else:
            pl.when(when)(one.start)
        sent[name, j] = waiting[name, j] = (one, when)

    def arrive(name, j):
        one, when = waiting.pop((name, j))
        if when is None:
            one.wait_recv()
        else:
            pl.when(when)(one.wait_recv)

    def leave(name, j):
        one, when = sent.pop((name, j))
        if when is None:
            one.wait_send()
        else:
            pl.when(when)(one.wait_send)

    def pair_out(name, j, buf, at, p, plus, minus):
        view = buf.at[rows_of(at + 2 * p, 2)]
        send(name + "p", j, view, view, plus)
        send(name + "m", j, view, view, minus)

    def pass_on(name, j, buf, at, before, after, q, plus, minus):
        up = buf.at[rows_of(at + 2 * before + q, 1)]
        down = buf.at[rows_of(at + 2 * after + 1 - q, 1)]
        send(name + "p", j, up, up, plus)
        send(name + "m", j, down, down, minus)

    def dressed_part(j, start):
        t = out[pl.ds(pl.multiple_of(start, half), half), :]
        return jnp.dot(t, bg[j][...], preferred_element_type=F32)

    def own_of(j):
        return p_own[j % OWN_SLOTS].at[:, pl.ds(0, WIDTHS[j])]

    def partial(j, block, count):
        at = rows_of(block, count)
        return own_of(j)[at] + sib[j][at].astype(F32)

    def set_gaps():
        gap[...] = 0.5 + 2.5 * jnp.sqrt(vir[...].astype(F32) / NVIR) + (
            0.5 + 2.5 * occ[...].astype(F32) / NOCC)
        blocks = 2 * half // 128

        def turn(i, carry):
            line = gap[pl.ds(c * blocks + i, 1), :]
            gap_rows[pl.ds(pl.multiple_of(i * 128, 128), 128), :] = jnp.broadcast_to(line, (128, 128)).T
            return carry
        lax.fori_loop(0, blocks, turn, 0)

    def product(j, part):
        tiles = half // GTILE // GPARTS

        def step(i, carry):
            h = i // 2 + part * tiles
            top = pl.multiple_of(i % 2 * half, half)
            at = pl.multiple_of(h * GTILE, GTILE)
            value = lax.dot_general(
                rows[j][pl.ds(top, half), :], cols[j][pl.ds(at, GTILE), :],
                (((1,), (1,)), ((), ())), preferred_element_type=F32)
            where = pl.ds(top, half), pl.ds(at, GTILE)
            if j == 0:
                acc[where] = value
            elif j < n - 1:
                acc[where] += value
            else:
                value = acc[where] + value
                for lane in range(0, GTILE, 128):
                    line = gap[pl.ds(r * (half // 128) + h * (GTILE // 128) + lane // 128, 1), :]
                    both = gap_rows[pl.ds(top, half), :] + line
                    out[pl.ds(top, half), pl.ds(at + lane, 128)] = (
                        -value[:, lane:lane + 128] / both).astype(BF16)
            return carry
        lax.fori_loop(0, 2 * tiles, step, 0)

    done = {}

    def run(name, j):
        own_a = rows_of(2 * z + yh, 1)
        own_c = rows_of(8 * k + 2 * here(x) + yl, 1)
        w = WIDTHS[j]
        columns = pl.ds(begin[j], w)
        if name == "ob1":
            send("ob1", 0, b_own, ob1r, mirror, mirrored)

            @pl.when(jnp.logical_not(mirrored))
            def _():
                ob1r[...] = b_own[...]
        elif name == "ob2":
            arrive("ob1", 0)
            send("ob2", 1, ob1r, ob2r, in_z, moves)

            @pl.when(jnp.logical_not(moves))
            def _():
                ob2r[...] = ob1r[...]
        elif name == "gap":
            set_gaps()
        elif name == "a1":
            send("a1", j, b_own.at[:, columns], bg[j].at[own_a], high)
            bg[j][own_a] = b_own[:, columns]
        elif name == "a2":
            arrive("a1", j)
            pair_out("a2", j, bg[j], 0, z, zp, zm)
        elif name == "a3":
            arrive("a2p", j)
            arrive("a2m", j)
            pass_on("a3", j, bg[j], 0, (z + 3) % 4, (z + 1) % 4, yh, zp, zm)
        elif name == "m1":
            arrive("a3p", j)
            arrive("a3m", j)
            if "t" not in done:
                t_copy.wait()
                done["t"] = True
            if j >= SEND_SLOTS:
                leave("dd", j - SEND_SLOTS)
            slot = p_send[j % SEND_SLOTS].at[:, pl.ds(0, w)]
            slot[...] = dressed_part(j, (1 - k) * half).astype(BF16)
            send("dd", j, slot, sib[j], other)
        elif name == "m2":
            own_of(j)[...] = dressed_part(j, k * half)
        elif name == "b1":
            arrive("dd", j)
            for side, (q, device) in enumerate(((yl, xp), (1 - yl, xm))):
                block = 2 * here(x + 2) + q
                sib[j][rows_of(block, 1)] = partial(j, block, 1).astype(BF16)
                send("b1" + "pm"[side], j, sib[j].at[rows_of(block, 1)], b1r[j].at[side], device)
        elif name == "b2":
            arrive("b1p", j)
            arrive("b1m", j)
            for side, (step, q, device) in enumerate(((1, yl, xp), (3, 1 - yl, xm))):
                first = 2 * here(x + step)
                one, two = rows_of(first + q, 1), rows_of(first + 1 - q, 1)
                sib[j][one] = (partial(j, first + q, 1) + b1r[j][side].astype(F32)).astype(BF16)
                sib[j][two] = partial(j, first + 1 - q, 1).astype(BF16)
                send("b2" + "pm"[side], j, sib[j].at[rows_of(first, 2)], b2r[j].at[side], device)
        elif name == "b3":
            arrive("b2p", j)
            arrive("b2m", j)

            def total(q):
                at = rows_of(q, 1)
                return partial(j, 2 * here(x) + q, 1) + (
                    b2r[j][0, at].astype(F32) + b2r[j][1, at].astype(F32))
            give = rows_of(2 * here(x) + 1 - yl, 1)
            sib[j][give] = total(1 - yl).astype(BF16)
            send("b3", j, sib[j].at[give], b3r[j], low)
            own_of(j)[rows_of(2 * here(x) + yl, 1)] = total(yl)
        elif name == "fin":
            if "b" not in done:
                arrive("ob2", 1)
                done["b"] = True
            arrive("b3", j)
            value = (own_of(j)[rows_of(2 * here(x) + yl, 1)] + b3r[j][...].astype(F32)
                     + ob2r[:, columns].astype(F32)).astype(BF16)
            rows[j][own_c] = value
            send("t1", j, rows[j].at[own_c], t1r[j], out_z, moves)
            send("c1", j, rows[j].at[own_c], rows[j].at[own_c], low)

            @pl.when(jnp.logical_not(moves))
            def _():
                t1r[j][...] = value
        elif name == "c2":
            arrive("c1", j)
            pair_out("c2", j, rows[j], 8 * k, here(x), xp, xm)
        elif name == "c3":
            arrive("c2p", j)
            arrive("c2m", j)
            pass_on("c3", j, rows[j], 8 * k, here(x + 3), here(x + 1), yl, xp, xm)
        elif name == "c4":
            arrive("c3p", j)
            arrive("c3m", j)
            mine = rows[j].at[rows_of(8 * k, 8)]
            send("c4", j, mine, mine, other)
        elif name == "t2":
            arrive("t1", j)
            at = rows_of(2 * z + yl, 1)
            send("t2", j, t1r[j], cols[j].at[at], mirror, mirrored)

            @pl.when(jnp.logical_not(mirrored))
            def _():
                cols[j][at] = t1r[j][...]
        elif name == "d1":
            arrive("t2", j)
            send("d1", j, cols[j].at[own_a], cols[j].at[own_a], high)
        elif name == "d2":
            arrive("d1", j)
            pair_out("d2", j, cols[j], 0, z, zp, zm)
        elif name == "d3":
            arrive("d2p", j)
            arrive("d2m", j)
            pass_on("d3", j, cols[j], 0, (z + 3) % 4, (z + 1) % 4, yh, zp, zm)
        elif name == "w":
            arrive("d3p", j)
            arrive("d3m", j)
            arrive("c4", j)
        elif name[0] == "g":
            product(j, int(name[1]))

    for name, j in ORDER:
        run(name, j)
    for name, j in list(sent):
        leave(name, j)


def update(amplitudes, cholesky, occ_map, vir_map):
    height, width = amplitudes.shape
    s, naux = cholesky.shape
    half = 8 * s
    n = len(WIDTHS)
    many = n * len(COPIES) + 2
    lines = occ_map.shape[0] // 128

    def each(*lead):
        return [pltpu.VMEM((*lead, w), BF16) for w in WIDTHS]

    vmem = pl.BlockSpec(memory_space=pltpu.VMEM)
    return pl.pallas_call(
        kernel,
        out_shape=pltpu.VMEM((height, width), BF16),
        in_specs=[pl.BlockSpec(memory_space=pl.ANY), vmem, vmem, vmem],
        out_specs=vmem,
        scratch_shapes=[
            each(8 * s),
            [pltpu.VMEM((half, max(WIDTHS)), BF16) for _ in range(SEND_SLOTS)],
            [pltpu.VMEM((half, max(WIDTHS)), F32) for _ in range(OWN_SLOTS)],
            each(half),
            each(2, s),
            each(2, 2 * s),
            each(s),
            each(2 * half),
            each(8 * s),
            each(s),
            pltpu.VMEM((s, naux), BF16),
            pltpu.VMEM((s, naux), BF16),
            pltpu.VMEM((height, width), F32),
            pltpu.VMEM((lines, 128), F32),
            pltpu.VMEM((height, 128), F32),
            pltpu.SemaphoreType.DMA((many,)),
            pltpu.SemaphoreType.DMA((many,)),
            pltpu.SemaphoreType.DMA((1,)),
        ],
        compiler_params=pltpu.CompilerParams(
            collective_id=0, has_side_effects=True, vmem_limit_bytes=53 * 2**20),
        cost_estimate=pl.CostEstimate(
            flops=4 * height * width * naux, bytes_accessed=4 * height * width, transcendentals=0),
    )(amplitudes, cholesky, occ_map.reshape(lines, 128), vir_map.reshape(lines, 128))


def solution(mesh):
    return jax.shard_map(
        update,
        mesh=mesh,
        in_specs=(P("col", "row"), P(("row", "col"), None), P(), P()),
        out_specs=P("col", "row"),
        check_vma=False,
    )
```

time: 156 us -> 150 us (0.962)
  matrix products: 18.7 us -> 0 us
  Pallas kernels: 133 us -> 145 us
  local copies, waits for them, and re-layouts: 0 us -> 3.74 us
    dot_general x1 -> x0, matrix products: 18.7 us -> none  [body(): lax.dot_general(rows, cols, (((1,), (1,)), ((), ())), preferred_element_t...]
    pallas_call x1, Pallas kernels: 133 us -> 145 us  [update(): pl.pallas_call(kernel, out_shape=pltpu.VMEM((height, width), BF16), in_sp...]
    unnamed x0 -> x1, local copies, waits for them, and re-layouts: none -> 3.74 us
where the time goes in v2:
time: 150 us; the launch traced here: 148 us
  Pallas kernels  145 us (97%)
  local copies, waits for them, and re-layouts  3.74 us (2%)
    pallas_call x1, Pallas kernels, update(): pl.pallas_call(kernel, out_shape=pltpu.VMEM((height, width), BF16), in_sp...  145 us
    unnamed x1, local copies, waits for them, and re-layouts  3.74 us

profile of v2, /device:TPU:1, one launch (start us, length us, event | category | flops | bytes accessed | tf_op | source)
XLA Modules:
  0.0 148.5 jit_solution(707671751166959895)
XLA Ops:
  0.0 144.7 %shard_map.46 = bf16[3072,1536]{1,0:T(8,128)(2,1)S(1)} custom-call(bf16[3072,1536]{1,0:T(8,128)(2,1)} %t_hbm.1, bf16[192,1280]{1,0:T(8,128)(2,1)} %b_own.1, s32[192,128]{1,0:T(8,128)} %bitcast.2, s32[192,128]{1,0:T(8,128)} %bitcast.3), custom_call_target="tpu_custom_call" | custom-call | flops 24159191040 | bytes 18874368 | tf_op jit(solution)/shard_map/pallas_call | solution.py:320
  144.7 3.7 %copy.6 = bf16[3072,1536]{1,0:T(8,128)(2,1)} copy(bf16[3072,1536]{1,0:T(8,128)(2,1)S(1)} %shard_map.46) | data formatting | bytes 18874368

commit v3 on v2

--- a/solution.py
+++ b/solution.py
@@ -11,25 +11,27 @@
 BF16 = jnp.bfloat16
 F32 = jnp.float32
 
-WIDTHS = [256, 256, 256, 256, 256]
+WIDTHS = [128, 256, 256, 256, 256, 128]
 OWN_SLOTS = 3
 SEND_SLOTS = 2
-GPARTS = 3
+GPARTS = 2
 GTILE = 256
 ORDER = [
-    ("a1", 0), ("a1", 1), ("gap", 0), ("a1", 2), ("ob1", 0), ("a1", 3), ("a1", 4), ("a2", 0),
-    ("a2", 1), ("a2", 2), ("a3", 0), ("a3", 1), ("a3", 2), ("ob2", 0), ("m1", 0), ("m2", 0),
-    ("m1", 1), ("b1", 0), ("m1", 2), ("m2", 1), ("b1", 1), ("m2", 2), ("b2", 0), ("b1", 2),
-    ("a2", 3), ("a2", 4), ("b2", 1), ("b3", 0), ("a3", 3), ("b2", 2), ("fin", 0), ("a3", 4),
-    ("b3", 1), ("m1", 3), ("m2", 3), ("t2", 0), ("b1", 3), ("fin", 1), ("b3", 2), ("m1", 4),
-    ("m2", 4), ("d1", 0), ("t2", 1), ("b1", 4), ("b2", 3), ("fin", 2), ("d2", 0), ("b2", 4),
-    ("d1", 1), ("t2", 2), ("c2", 0), ("c2", 1), ("c2", 2), ("b3", 3), ("d2", 1), ("d3", 0),
-    ("b3", 4), ("fin", 3), ("d1", 2), ("d3", 1), ("fin", 4), ("c3", 0), ("t2", 3), ("c2", 3),
-    ("d2", 2), ("t2", 4), ("c3", 1), ("c2", 4), ("c3", 2), ("d3", 2), ("c4", 0), ("d1", 3),
-    ("w", 0), ("g2", 0), ("g1", 0), ("g0", 0), ("d2", 3), ("c3", 3), ("d1", 4), ("c4", 1),
-    ("d2", 4), ("w", 1), ("g2", 1), ("d3", 3), ("g1", 1), ("g0", 1), ("c3", 4), ("c4", 2),
-    ("d3", 4), ("w", 2), ("g2", 2), ("c4", 3), ("g1", 2), ("c4", 4), ("g0", 2), ("w", 3),
-    ("g2", 3), ("g1", 3), ("g0", 3), ("w", 4), ("g2", 4), ("g1", 4), ("g0", 4),
+    ("a1", 0), ("a1", 2), ("a1", 3), ("a1", 1), ("a2", 0), ("a1", 4), ("a1", 5), ("a2", 2),
+    ("a3", 0), ("a2", 1), ("a3", 2), ("m1", 0), ("m2", 0), ("b1", 0), ("a3", 1), ("a2", 3),
+    ("a2", 5), ("m1", 2), ("b2", 0), ("m2", 2), ("m1", 1), ("b1", 2), ("m2", 1), ("b1", 1),
+    ("b3", 0), ("a3", 3), ("a2", 4), ("b2", 2), ("m1", 3), ("fin", 0), ("a3", 5), ("b2", 1),
+    ("m2", 3), ("b3", 2), ("b1", 3), ("gap", 0), ("t2", 0), ("c2", 0), ("a3", 4), ("m1", 5),
+    ("b3", 1), ("fin", 2), ("b2", 3), ("d1", 0), ("m2", 5), ("fin", 1), ("c3", 0), ("m1", 4),
+    ("m2", 4), ("b1", 5), ("b1", 4), ("d2", 0), ("t2", 2), ("t2", 1), ("b3", 3), ("d3", 0),
+    ("b2", 5), ("d1", 2), ("fin", 3), ("b2", 4), ("c2", 2), ("c4", 0), ("b3", 5), ("fin", 5),
+    ("b3", 4), ("d1", 1), ("d2", 2), ("c2", 1), ("t2", 3), ("fin", 4), ("t2", 5), ("d2", 1),
+    ("c3", 1), ("t2", 4), ("c3", 2), ("w", 0), ("c2", 3), ("d1", 3), ("d3", 2), ("g0", 0),
+    ("c2", 4), ("d3", 1), ("d1", 5), ("c4", 1), ("g1", 0), ("d1", 4), ("d2", 3), ("c4", 2),
+    ("d2", 4), ("w", 1), ("w", 2), ("c3", 3), ("c2", 5), ("g0", 1), ("g0", 2), ("d3", 3),
+    ("d2", 5), ("g1", 1), ("c3", 4), ("c4", 3), ("d3", 4), ("g1", 2), ("w", 3), ("c3", 5),
+    ("g0", 3), ("d3", 5), ("c4", 4), ("g1", 3), ("c4", 5), ("w", 4), ("g1", 4), ("w", 5),
+    ("g0", 4), ("g0", 5), ("g1", 5),
 ]
 
 COPIES = [
@@ -43,7 +45,7 @@
 
 
 def kernel(t_hbm, b_own, occ, vir, out, bg, p_send, p_own, sib, b1r, b2r, b3r, rows, cols, t1r,
-           ob1r, ob2r, acc, gap, gap_rows, send_sem, recv_sem, local_sem):
+           acc, gap, gap_rows, send_sem, recv_sem, local_sem):
     r, c = lax.axis_index("row"), lax.axis_index("col")
     x, yl, k = r // 4, (r // 2) % 2, r % 2
     z, yh = c // 2, c % 2
@@ -68,8 +70,7 @@
 
     @pl.when(moves)
     def _():
-        for device in (out_z, in_z):
-            pl.semaphore_signal(barrier, inc=1, device_id=device, device_id_type=MESH)
+        pl.semaphore_signal(barrier, inc=1, device_id=in_z, device_id_type=MESH)
 
     @pl.when(mirrored)
     def _():
@@ -78,10 +79,10 @@
     t_copy = pltpu.make_async_copy(t_hbm, out, local_sem.at[0])
     t_copy.start()
 
-    pl.semaphore_wait(barrier, 7 + 2 * moves.astype(jnp.int32) + mirrored.astype(jnp.int32))
+    pl.semaphore_wait(barrier, 7 + moves.astype(jnp.int32) + mirrored.astype(jnp.int32))
 
     def copy(name, j, src, dst, device):
-        at = j * len(COPIES) + COPIES.index(name) if name in COPIES else n * len(COPIES) + j
+        at = j * len(COPIES) + COPIES.index(name)
         return pltpu.make_async_remote_copy(
             src_ref=src, dst_ref=dst, send_sem=send_sem.at[at], recv_sem=recv_sem.at[at],
             device_id=device, device_id_type=MESH,
@@ -152,29 +153,29 @@
         lax.fori_loop(0, blocks, turn, 0)
 
     def product(j, part):
-        tiles = half // GTILE // GPARTS
+        tiles = acc.shape[0] // GPARTS
 
         def step(i, carry):
-            h = i // 2 + part * tiles
-            top = pl.multiple_of(i % 2 * half, half)
-            at = pl.multiple_of(h * GTILE, GTILE)
-            value = lax.dot_general(
-                rows[j][pl.ds(top, half), :], cols[j][pl.ds(at, GTILE), :],
-                (((1,), (1,)), ((), ())), preferred_element_type=F32)
-            where = pl.ds(top, half), pl.ds(at, GTILE)
-            if j == 0:
-                acc[where] = value
-            elif j < n - 1:
-                acc[where] += value
-            else:
-                value = acc[where] + value
-                for lane in range(0, GTILE, 128):
-                    line = gap[pl.ds(r * (half // 128) + h * (GTILE // 128) + lane // 128, 1), :]
-                    both = gap_rows[pl.ds(top, half), :] + line
-                    out[pl.ds(top, half), pl.ds(at + lane, 128)] = (
-                        -value[:, lane:lane + 128] / both).astype(BF16)
+            down = pl.ds(pl.multiple_of(i * half, half), half)
+            left = rows[j][down, :]
+            for h in range(part * tiles, (part + 1) * tiles):
+                at = h * GTILE
+                value = lax.dot_general(
+                    left, cols[j][at:at + GTILE, :],
+                    (((1,), (1,)), ((), ())), preferred_element_type=F32)
+                if j == 0:
+                    acc[h, down] = value
+                elif j < n - 1:
+                    acc[h, down] += value
+                else:
+                    value = acc[h, down] + value
+                    for lane in range(0, GTILE, 128):
+                        line = gap[pl.ds(r * (half // 128) + (at + lane) // 128, 1), :]
+                        both = gap_rows[down, :] + line
+                        out[down, at + lane:at + lane + 128] = (
+                            -value[:, lane:lane + 128] / both).astype(BF16)
             return carry
-        lax.fori_loop(0, 2 * tiles, step, 0)
+        lax.fori_loop(0, 2, step, 0)
 
     done = {}
 
@@ -183,20 +184,7 @@
         own_c = rows_of(8 * k + 2 * here(x) + yl, 1)
         w = WIDTHS[j]
         columns = pl.ds(begin[j], w)
-        if name == "ob1":
-            send("ob1", 0, b_own, ob1r, mirror, mirrored)
-
-            @pl.when(jnp.logical_not(mirrored))
-            def _():
-                ob1r[...] = b_own[...]
-        elif name == "ob2":
-            arrive("ob1", 0)
-            send("ob2", 1, ob1r, ob2r, in_z, moves)
-
-            @pl.when(jnp.logical_not(moves))
-            def _():
-                ob2r[...] = ob1r[...]
-        elif name == "gap":
+        if name == "gap":
             set_gaps()
         elif name == "a1":
             send("a1", j, b_own.at[:, columns], bg[j].at[own_a], high)
@@ -221,6 +209,10 @@
             send("dd", j, slot, sib[j], other)
         elif name == "m2":
             own_of(j)[...] = dressed_part(j, k * half)
+
+            @pl.when(jnp.logical_and(x == z, yl == yh))
+            def _():
+                own_of(j)[...] += bg[j][...].astype(F32)
         elif name == "b1":
             arrive("dd", j)
             for side, (q, device) in enumerate(((yl, xp), (1 - yl, xm))):
@@ -249,12 +241,9 @@
             send("b3", j, sib[j].at[give], b3r[j], low)
             own_of(j)[rows_of(2 * here(x) + yl, 1)] = total(yl)
         elif name == "fin":
-            if "b" not in done:
-                arrive("ob2", 1)
-                done["b"] = True
             arrive("b3", j)
-            value = (own_of(j)[rows_of(2 * here(x) + yl, 1)] + b3r[j][...].astype(F32)
-                     + ob2r[:, columns].astype(F32)).astype(BF16)
+            kept = own_of(j)[rows_of(2 * here(x) + yl, 1)]
+            value = (kept + b3r[j][...].astype(F32)).astype(BF16)
             rows[j][own_c] = value
             send("t1", j, rows[j].at[own_c], t1r[j], out_z, moves)
             send("c1", j, rows[j].at[own_c], rows[j].at[own_c], low)
@@ -310,7 +299,7 @@
     s, naux = cholesky.shape
     half = 8 * s
     n = len(WIDTHS)
-    many = n * len(COPIES) + 2
+    many = n * len(COPIES)
     lines = occ_map.shape[0] // 128
 
     def each(*lead):
@@ -333,9 +322,7 @@
             each(2 * half),
             each(8 * s),
             each(s),
-            pltpu.VMEM((s, naux), BF16),
-            pltpu.VMEM((s, naux), BF16),
-            pltpu.VMEM((height, width), F32),
+            pltpu.VMEM((width // GTILE, height, GTILE), F32),
             pltpu.VMEM((lines, 128), F32),
             pltpu.VMEM((height, 128), F32),
             pltpu.SemaphoreType.DMA((many,)),

time: 150 us -> 133 us (0.89); the launches traced: 148 us -> 133 us
  Pallas kernels: 145 us -> 129 us
    pallas_call x1, Pallas kernels: 145 us -> 129 us  [update(): pl.pallas_call(kernel, out_shape=pltpu.VMEM((height, width), BF16), in_sp...]
where the time goes in v3:
time: 133 us
  Pallas kernels  129 us (97%)
  local copies, waits for them, and re-layouts  3.74 us (3%)
    pallas_call x1, Pallas kernels, update(): pl.pallas_call(kernel, out_shape=pltpu.VMEM((height, width), BF16), in_sp...  129 us
    unnamed x1, local copies, waits for them, and re-layouts  3.74 us

profile of v3, /device:TPU:1, one launch (start us, length us, event | category | flops | bytes accessed | tf_op | source)
XLA Modules:
  0.0 133.2 jit_solution(2078663299516082790)
XLA Ops:
  0.0 129.4 %shard_map.46 = bf16[3072,1536]{1,0:T(8,128)(2,1)S(1)} custom-call(bf16[3072,1536]{1,0:T(8,128)(2,1)} %t_hbm.1, bf16[192,1280]{1,0:T(8,128)(2,1)} %b_own.1, s32[192,128]{1,0:T(8,128)} %bitcast.2, s32[192,128]{1,0:T(8,128)} %bitcast.3), custom_call_target="tpu_custom_call" | custom-call | flops 24159191040 | bytes 18874368 | tf_op jit(solution)/shard_map/pallas_call | solution.py:309
  129.4 3.7 %copy.6 = bf16[3072,1536]{1,0:T(8,128)(2,1)} copy(bf16[3072,1536]{1,0:T(8,128)(2,1)S(1)} %shard_map.46) | data formatting | bytes 18874368

commit v4 on v3

--- a/solution.py
+++ b/solution.py
@@ -12,31 +12,36 @@
 F32 = jnp.float32
 
 WIDTHS = [128, 256, 256, 256, 256, 128]
+A_LATE = (1, )
+C_LATE = (3, 4, )
+D_LATE = (4, )
 OWN_SLOTS = 3
 SEND_SLOTS = 2
 GPARTS = 2
 GTILE = 256
 ORDER = [
-    ("a1", 0), ("a1", 2), ("a1", 3), ("a1", 1), ("a2", 0), ("a1", 4), ("a1", 5), ("a2", 2),
-    ("a3", 0), ("a2", 1), ("a3", 2), ("m1", 0), ("m2", 0), ("b1", 0), ("a3", 1), ("a2", 3),
-    ("a2", 5), ("m1", 2), ("b2", 0), ("m2", 2), ("m1", 1), ("b1", 2), ("m2", 1), ("b1", 1),
-    ("b3", 0), ("a3", 3), ("a2", 4), ("b2", 2), ("m1", 3), ("fin", 0), ("a3", 5), ("b2", 1),
-    ("m2", 3), ("b3", 2), ("b1", 3), ("gap", 0), ("t2", 0), ("c2", 0), ("a3", 4), ("m1", 5),
-    ("b3", 1), ("fin", 2), ("b2", 3), ("d1", 0), ("m2", 5), ("fin", 1), ("c3", 0), ("m1", 4),
-    ("m2", 4), ("b1", 5), ("b1", 4), ("d2", 0), ("t2", 2), ("t2", 1), ("b3", 3), ("d3", 0),
-    ("b2", 5), ("d1", 2), ("fin", 3), ("b2", 4), ("c2", 2), ("c4", 0), ("b3", 5), ("fin", 5),
-    ("b3", 4), ("d1", 1), ("d2", 2), ("c2", 1), ("t2", 3), ("fin", 4), ("t2", 5), ("d2", 1),
-    ("c3", 1), ("t2", 4), ("c3", 2), ("w", 0), ("c2", 3), ("d1", 3), ("d3", 2), ("g0", 0),
-    ("c2", 4), ("d3", 1), ("d1", 5), ("c4", 1), ("g1", 0), ("d1", 4), ("d2", 3), ("c4", 2),
-    ("d2", 4), ("w", 1), ("w", 2), ("c3", 3), ("c2", 5), ("g0", 1), ("g0", 2), ("d3", 3),
-    ("d2", 5), ("g1", 1), ("c3", 4), ("c4", 3), ("d3", 4), ("g1", 2), ("w", 3), ("c3", 5),
-    ("g0", 3), ("d3", 5), ("c4", 4), ("g1", 3), ("c4", 5), ("w", 4), ("g1", 4), ("w", 5),
-    ("g0", 4), ("g0", 5), ("g1", 5),
+    ("a1", 0), ("a1", 2), ("a1", 1), ("a2", 0), ("a2", 1), ("a1", 3), ("a3", 0), ("a2", 2),
+    ("a3", 1), ("m1", 0), ("m2", 0), ("a1", 4), ("b1", 0), ("a1", 5), ("a3", 2), ("m1", 1),
+    ("a2", 3), ("b2", 0), ("m2", 1), ("b1", 1), ("m1", 2), ("m2", 2), ("b1", 2), ("b3", 0),
+    ("a3", 3), ("b2", 1), ("a2", 4), ("fin", 0), ("b2", 2), ("m1", 3), ("m2", 3), ("b1", 3),
+    ("a2", 5), ("t2", 0), ("b3", 1), ("a3", 4), ("c2", 0), ("b2", 3), ("fin", 1), ("m1", 4),
+    ("b3", 2), ("a3", 5), ("m2", 4), ("b1", 4), ("c3", 0), ("m1", 5), ("d1", 0), ("fin", 2),
+    ("t2", 1), ("m2", 5), ("b3", 3), ("b1", 5), ("b2", 4), ("t2", 2), ("d2", 0), ("b2", 5),
+    ("d1", 1), ("fin", 3), ("t2", 3), ("b3", 4), ("d2", 1), ("d1", 2), ("c2", 1), ("b3", 5),
+    ("fin", 4), ("d3", 0), ("d1", 3), ("c2", 3), ("t2", 4), ("c4", 0), ("fin", 5), ("d3", 1),
+    ("w", 0), ("d2", 2), ("g1", 0), ("c2", 2), ("c3", 3), ("d1", 4), ("c3", 1), ("t2", 5),
+    ("c2", 4), ("d2", 3), ("gap", 0), ("g0", 0), ("c3", 2), ("c4", 1), ("d3", 2), ("c2", 5),
+    ("d1", 5), ("d2", 4), ("c4", 3), ("w", 1), ("g0", 1), ("d3", 3), ("c3", 4), ("c4", 2),
+    ("g1", 1), ("d3", 4), ("d2", 5), ("c3", 5), ("w", 2), ("g0", 2), ("g1", 2), ("w", 3),
+    ("g1", 3), ("c4", 4), ("g0", 3), ("d3", 5), ("c4", 5), ("w", 4), ("g0", 4), ("g1", 4),
+    ("w", 5), ("g1", 5), ("g0", 5),
 ]
 
 COPIES = [
     "a1", "a2p", "a2m", "a3p", "a3m", "dd", "b1p", "b1m", "b2p", "b2m", "b3",
     "c1", "c2p", "c2m", "c3p", "c3m", "c4", "t1", "t2", "d1", "d2p", "d2m", "d3p", "d3m",
+    "a1p", "a1m", "a1y", "a2u", "a2v", "a3y", "c1p", "c1m", "c1y", "c2u", "c2v", "c3y",
+    "d1p", "d1m", "d1y", "d2u", "d2v", "d3y",
 ]
 
 
@@ -129,6 +134,29 @@
         down = buf.at[rows_of(at + 2 * after + 1 - q, 1)]
         send(name + "p", j, up, up, plus)
         send(name + "m", j, down, down, minus)
+
+    def late_first(name, j, src, view, plus, minus, partner):
+        for end, device in zip("pmy", (plus, minus, partner)):
+            send(name + "1" + end, j, src, view, device)
+
+    def late_second(name, j, buf, at, before, after, q, plus, minus, partner):
+        for end, pos, shift, device, also in (("p", before, 0, plus, "u"), ("m", after, 1, minus, "v")):
+            arrive(name + "1" + end, j)
+            first = (at + 2 * pos + q) * s
+            part = buf.at[pl.ds(pl.multiple_of(first + shift * s // 2, s // 2), s // 2)]
+            send(name + "2" + end, j, part, part, device)
+            whole = buf.at[pl.ds(pl.multiple_of(first, s), s)]
+            send(name + "2" + also, j, whole, whole, partner)
+
+    def late_third(name, j, buf, at, far, q, partner):
+        arrive(name + "2p", j)
+        arrive(name + "2m", j)
+        view = buf.at[rows_of(at + 2 * far + q, 1)]
+        send(name + "3y", j, view, view, partner)
+
+    def gathered(name, j, late):
+        for end in ("1y", "2u", "2v", "3y") if late else ("3p", "3m"):
+            arrive(name + end, j)
 
     def dressed_part(j, start):
         t = out[pl.ds(pl.multiple_of(start, half), half), :]
@@ -187,18 +215,27 @@
         if name == "gap":
             set_gaps()
         elif name == "a1":
-            send("a1", j, b_own.at[:, columns], bg[j].at[own_a], high)
+            src, view = b_own.at[:, columns], bg[j].at[own_a]
+            if j in A_LATE:
+                late_first("a", j, src, view, zp, zm, high)
+            else:
+                send("a1", j, src, view, high)
             bg[j][own_a] = b_own[:, columns]
         elif name == "a2":
-            arrive("a1", j)
-            pair_out("a2", j, bg[j], 0, z, zp, zm)
+            if j in A_LATE:
+                late_second("a", j, bg[j], 0, (z + 3) % 4, (z + 1) % 4, yh, zp, zm, high)
+            else:
+                arrive("a1", j)
+                pair_out("a2", j, bg[j], 0, z, zp, zm)
         elif name == "a3":
+            if j in A_LATE:
+                late_third("a", j, bg[j], 0, (z + 2) % 4, yh, high)
+                return
             arrive("a2p", j)
             arrive("a2m", j)
             pass_on("a3", j, bg[j], 0, (z + 3) % 4, (z + 1) % 4, yh, zp, zm)
         elif name == "m1":
-            arrive("a3p", j)
-            arrive("a3m", j)
+            gathered("a", j, j in A_LATE)
             if "t" not in done:
                 t_copy.wait()
                 done["t"] = True
@@ -246,21 +283,30 @@
             value = (kept + b3r[j][...].astype(F32)).astype(BF16)
             rows[j][own_c] = value
             send("t1", j, rows[j].at[own_c], t1r[j], out_z, moves)
-            send("c1", j, rows[j].at[own_c], rows[j].at[own_c], low)
+            view = rows[j].at[own_c]
+            if j in C_LATE:
+                late_first("c", j, view, view, xp, xm, low)
+            else:
+                send("c1", j, view, view, low)
 
             @pl.when(jnp.logical_not(moves))
             def _():
                 t1r[j][...] = value
         elif name == "c2":
-            arrive("c1", j)
-            pair_out("c2", j, rows[j], 8 * k, here(x), xp, xm)
+            if j in C_LATE:
+                late_second("c", j, rows[j], 8 * k, here(x + 3), here(x + 1), yl, xp, xm, low)
+            else:
+                arrive("c1", j)
+                pair_out("c2", j, rows[j], 8 * k, here(x), xp, xm)
         elif name == "c3":
+            if j in C_LATE:
+                late_third("c", j, rows[j], 8 * k, here(x + 2), yl, low)
+                return
             arrive("c2p", j)
             arrive("c2m", j)
             pass_on("c3", j, rows[j], 8 * k, here(x + 3), here(x + 1), yl, xp, xm)
         elif name == "c4":
-            arrive("c3p", j)
-            arrive("c3m", j)
+            gathered("c", j, j in C_LATE)
             mine = rows[j].at[rows_of(8 * k, 8)]
             send("c4", j, mine, mine, other)
         elif name == "t2":
@@ -273,17 +319,26 @@
                 cols[j][at] = t1r[j][...]
         elif name == "d1":
             arrive("t2", j)
-            send("d1", j, cols[j].at[own_a], cols[j].at[own_a], high)
+            view = cols[j].at[own_a]
+            if j in D_LATE:
+                late_first("d", j, view, view, zp, zm, high)
+            else:
+                send("d1", j, view, view, high)
         elif name == "d2":
-            arrive("d1", j)
-            pair_out("d2", j, cols[j], 0, z, zp, zm)
+            if j in D_LATE:
+                late_second("d", j, cols[j], 0, (z + 3) % 4, (z + 1) % 4, yh, zp, zm, high)
+            else:
+                arrive("d1", j)
+                pair_out("d2", j, cols[j], 0, z, zp, zm)
         elif name == "d3":
+            if j in D_LATE:
+                late_third("d", j, cols[j], 0, (z + 2) % 4, yh, high)
+                return
             arrive("d2p", j)
             arrive("d2m", j)
             pass_on("d3", j, cols[j], 0, (z + 3) % 4, (z + 1) % 4, yh, zp, zm)
         elif name == "w":
-            arrive("d3p", j)
-            arrive("d3m", j)
+            gathered("d", j, j in D_LATE)
             arrive("c4", j)
         elif name[0] == "g":
             product(j, int(name[1]))

time: 133 us -> 129 us (0.970)
  Pallas kernels: 129 us -> 125 us
    pallas_call x1, Pallas kernels: 129 us -> 125 us  [update(): pl.pallas_call(kernel, out_shape=pltpu.VMEM((height, width), BF16), in_sp...]
where the time goes in v4:
time: 129 us
  Pallas kernels  125 us (97%)
  local copies, waits for them, and re-layouts  3.74 us (3%)
    pallas_call x1, Pallas kernels, update(): pl.pallas_call(kernel, out_shape=pltpu.VMEM((height, width), BF16), in_sp...  125 us
    unnamed x1, local copies, waits for them, and re-layouts  3.74 us

profile of v4, /device:TPU:1, one launch (start us, length us, event | category | flops | bytes accessed | tf_op | source)
XLA Modules:
  0.0 129.1 jit_solution(15568807625661023788)
XLA Ops:
  0.0 125.3 %shard_map.46 = bf16[3072,1536]{1,0:T(8,128)(2,1)S(1)} custom-call(bf16[3072,1536]{1,0:T(8,128)(2,1)} %t_hbm.1, bf16[192,1280]{1,0:T(8,128)(2,1)} %b_own.1, s32[192,128]{1,0:T(8,128)} %bitcast.2, s32[192,128]{1,0:T(8,128)} %bitcast.3), custom_call_target="tpu_custom_call" | custom-call | flops 24159191040 | bytes 18874368 | tf_op jit(solution)/shard_map/pallas_call | solution.py:364
  125.3 3.7 %copy.6 = bf16[3072,1536]{1,0:T(8,128)(2,1)} copy(bf16[3072,1536]{1,0:T(8,128)(2,1)S(1)} %shard_map.46) | data formatting | bytes 18874368

commit v5 on v4

--- a/solution.py
+++ b/solution.py
@@ -13,28 +13,28 @@
 
 WIDTHS = [128, 256, 256, 256, 256, 128]
 A_LATE = (1, )
-C_LATE = (3, 4, )
+C_LATE = (2, 4, )
 D_LATE = (4, )
 OWN_SLOTS = 3
 SEND_SLOTS = 2
 GPARTS = 2
 GTILE = 256
 ORDER = [
-    ("a1", 0), ("a1", 2), ("a1", 1), ("a2", 0), ("a2", 1), ("a1", 3), ("a3", 0), ("a2", 2),
-    ("a3", 1), ("m1", 0), ("m2", 0), ("a1", 4), ("b1", 0), ("a1", 5), ("a3", 2), ("m1", 1),
-    ("a2", 3), ("b2", 0), ("m2", 1), ("b1", 1), ("m1", 2), ("m2", 2), ("b1", 2), ("b3", 0),
-    ("a3", 3), ("b2", 1), ("a2", 4), ("fin", 0), ("b2", 2), ("m1", 3), ("m2", 3), ("b1", 3),
-    ("a2", 5), ("t2", 0), ("b3", 1), ("a3", 4), ("c2", 0), ("b2", 3), ("fin", 1), ("m1", 4),
-    ("b3", 2), ("a3", 5), ("m2", 4), ("b1", 4), ("c3", 0), ("m1", 5), ("d1", 0), ("fin", 2),
-    ("t2", 1), ("m2", 5), ("b3", 3), ("b1", 5), ("b2", 4), ("t2", 2), ("d2", 0), ("b2", 5),
-    ("d1", 1), ("fin", 3), ("t2", 3), ("b3", 4), ("d2", 1), ("d1", 2), ("c2", 1), ("b3", 5),
-    ("fin", 4), ("d3", 0), ("d1", 3), ("c2", 3), ("t2", 4), ("c4", 0), ("fin", 5), ("d3", 1),
-    ("w", 0), ("d2", 2), ("g1", 0), ("c2", 2), ("c3", 3), ("d1", 4), ("c3", 1), ("t2", 5),
-    ("c2", 4), ("d2", 3), ("gap", 0), ("g0", 0), ("c3", 2), ("c4", 1), ("d3", 2), ("c2", 5),
-    ("d1", 5), ("d2", 4), ("c4", 3), ("w", 1), ("g0", 1), ("d3", 3), ("c3", 4), ("c4", 2),
-    ("g1", 1), ("d3", 4), ("d2", 5), ("c3", 5), ("w", 2), ("g0", 2), ("g1", 2), ("w", 3),
-    ("g1", 3), ("c4", 4), ("g0", 3), ("d3", 5), ("c4", 5), ("w", 4), ("g0", 4), ("g1", 4),
-    ("w", 5), ("g1", 5), ("g0", 5),
+    ("a1", 0), ("a1", 1), ("a1", 2), ("a2", 0), ("a1", 3), ("a2", 1), ("a3", 0), ("a2", 2),
+    ("a3", 1), ("m1", 0), ("m2", 0), ("a1", 4), ("b1", 0), ("a3", 2), ("a2", 3), ("m1", 1),
+    ("m2", 1), ("b2", 0), ("b1", 1), ("a2", 4), ("m1", 2), ("m2", 2), ("b1", 2), ("b3", 0),
+    ("a1", 5), ("a3", 3), ("b2", 1), ("b2", 2), ("a3", 4), ("fin", 0), ("m1", 3), ("a2", 5),
+    ("m2", 3), ("b3", 1), ("b1", 3), ("t2", 0), ("c2", 0), ("m1", 4), ("b3", 2), ("b2", 3),
+    ("fin", 1), ("m2", 4), ("d1", 0), ("b1", 4), ("fin", 2), ("t2", 1), ("a3", 5), ("d2", 0),
+    ("t2", 2), ("b3", 3), ("m1", 5), ("m2", 5), ("b1", 5), ("fin", 3), ("d1", 1), ("c3", 0),
+    ("b2", 4), ("d1", 2), ("b2", 5), ("d3", 0), ("c4", 0), ("t2", 3), ("c2", 1), ("c2", 2),
+    ("d2", 1), ("d2", 2), ("w", 0), ("b3", 4), ("g0", 0), ("d1", 3), ("b3", 5), ("fin", 4),
+    ("d3", 1), ("c3", 1), ("fin", 5), ("c3", 2), ("d2", 3), ("d3", 2), ("t2", 4), ("c2", 4),
+    ("c2", 3), ("g1", 0), ("c4", 1), ("gap", 0), ("t2", 5), ("c4", 2), ("d1", 4), ("w", 1),
+    ("c3", 4), ("g0", 1), ("c2", 5), ("g1", 1), ("d3", 3), ("c3", 3), ("w", 2), ("d1", 5),
+    ("d2", 4), ("g0", 2), ("g1", 2), ("c4", 3), ("c4", 4), ("d2", 5), ("d3", 4), ("c3", 5),
+    ("w", 3), ("g0", 3), ("g1", 3), ("c4", 5), ("d3", 5), ("w", 4), ("g0", 4), ("g1", 4),
+    ("w", 5), ("g0", 5), ("g1", 5),
 ]
 
 COPIES = [

time: 129 us -> 124 us (0.961)
  Pallas kernels: 125 us -> 120 us
    pallas_call x1, Pallas kernels: 125 us -> 120 us  [update(): pl.pallas_call(kernel, out_shape=pltpu.VMEM((height, width), BF16), in_sp...]
where the time goes in v5:
time: 124 us; the launch traced here: 123 us
  Pallas kernels  120 us (97%)
  local copies, waits for them, and re-layouts  3.74 us (3%)
    pallas_call x1, Pallas kernels, update(): pl.pallas_call(kernel, out_shape=pltpu.VMEM((height, width), BF16), in_sp...  120 us
    unnamed x1, local copies, waits for them, and re-layouts  3.74 us

profile of v5, /device:TPU:1, one launch (start us, length us, event | category | flops | bytes accessed | tf_op | source)
XLA Modules:
  0.0 123.5 jit_solution(3773540699183158743)
XLA Ops:
  0.0 119.7 %shard_map.46 = bf16[3072,1536]{1,0:T(8,128)(2,1)S(1)} custom-call(bf16[3072,1536]{1,0:T(8,128)(2,1)} %t_hbm.1, bf16[192,1280]{1,0:T(8,128)(2,1)} %b_own.1, s32[192,128]{1,0:T(8,128)} %bitcast.2, s32[192,128]{1,0:T(8,128)} %bitcast.3), custom_call_target="tpu_custom_call" | custom-call | flops 24159191040 | bytes 18874368 | tf_op jit(solution)/shard_map/pallas_call | solution.py:364
  119.7 3.7 %copy.6 = bf16[3072,1536]{1,0:T(8,128)(2,1)} copy(bf16[3072,1536]{1,0:T(8,128)(2,1)S(1)} %shard_map.46) | data formatting | bytes 18874368

commit v6 on v5

--- a/solution.py
+++ b/solution.py
@@ -13,28 +13,28 @@
 
 WIDTHS = [128, 256, 256, 256, 256, 128]
 A_LATE = (1, )
-C_LATE = (2, 4, )
+C_LATE = (2, 3, 4, )
 D_LATE = (4, )
 OWN_SLOTS = 3
 SEND_SLOTS = 2
 GPARTS = 2
 GTILE = 256
 ORDER = [
-    ("a1", 0), ("a1", 1), ("a1", 2), ("a2", 0), ("a1", 3), ("a2", 1), ("a3", 0), ("a2", 2),
-    ("a3", 1), ("m1", 0), ("m2", 0), ("a1", 4), ("b1", 0), ("a3", 2), ("a2", 3), ("m1", 1),
-    ("m2", 1), ("b2", 0), ("b1", 1), ("a2", 4), ("m1", 2), ("m2", 2), ("b1", 2), ("b3", 0),
-    ("a1", 5), ("a3", 3), ("b2", 1), ("b2", 2), ("a3", 4), ("fin", 0), ("m1", 3), ("a2", 5),
-    ("m2", 3), ("b3", 1), ("b1", 3), ("t2", 0), ("c2", 0), ("m1", 4), ("b3", 2), ("b2", 3),
-    ("fin", 1), ("m2", 4), ("d1", 0), ("b1", 4), ("fin", 2), ("t2", 1), ("a3", 5), ("d2", 0),
-    ("t2", 2), ("b3", 3), ("m1", 5), ("m2", 5), ("b1", 5), ("fin", 3), ("d1", 1), ("c3", 0),
-    ("b2", 4), ("d1", 2), ("b2", 5), ("d3", 0), ("c4", 0), ("t2", 3), ("c2", 1), ("c2", 2),
-    ("d2", 1), ("d2", 2), ("w", 0), ("b3", 4), ("g0", 0), ("d1", 3), ("b3", 5), ("fin", 4),
-    ("d3", 1), ("c3", 1), ("fin", 5), ("c3", 2), ("d2", 3), ("d3", 2), ("t2", 4), ("c2", 4),
-    ("c2", 3), ("g1", 0), ("c4", 1), ("gap", 0), ("t2", 5), ("c4", 2), ("d1", 4), ("w", 1),
-    ("c3", 4), ("g0", 1), ("c2", 5), ("g1", 1), ("d3", 3), ("c3", 3), ("w", 2), ("d1", 5),
-    ("d2", 4), ("g0", 2), ("g1", 2), ("c4", 3), ("c4", 4), ("d2", 5), ("d3", 4), ("c3", 5),
-    ("w", 3), ("g0", 3), ("g1", 3), ("c4", 5), ("d3", 5), ("w", 4), ("g0", 4), ("g1", 4),
-    ("w", 5), ("g0", 5), ("g1", 5),
+    ("a1", 0), ("a1", 1), ("a1", 2), ("a2", 0), ("a2", 1), ("a3", 0), ("a1", 3), ("a2", 2),
+    ("a3", 1), ("m1", 0), ("a1", 5), ("m2", 0), ("b1", 0), ("a3", 2), ("a2", 3), ("m1", 1),
+    ("m2", 1), ("b1", 1), ("a1", 4), ("a2", 5), ("b2", 0), ("m1", 2), ("m2", 2), ("b1", 2),
+    ("a3", 3), ("a2", 4), ("b2", 1), ("a3", 5), ("b3", 0), ("b2", 2), ("m1", 3), ("fin", 0),
+    ("m2", 3), ("b3", 1), ("b1", 3), ("t2", 0), ("c2", 0), ("a3", 4), ("b3", 2), ("b2", 3),
+    ("fin", 1), ("m1", 4), ("fin", 2), ("d1", 0), ("m2", 4), ("t2", 1), ("b1", 4), ("m1", 5),
+    ("b3", 3), ("m2", 5), ("b1", 5), ("t2", 2), ("c2", 2), ("d1", 1), ("d2", 0), ("b2", 5),
+    ("b2", 4), ("fin", 3), ("d3", 0), ("d1", 2), ("b3", 5), ("c3", 2), ("c3", 0), ("d2", 1),
+    ("d2", 2), ("t2", 3), ("fin", 5), ("b3", 4), ("c2", 1), ("c2", 3), ("c4", 0), ("gap", 0),
+    ("d1", 3), ("fin", 4), ("d3", 1), ("w", 0), ("g1", 0), ("d3", 2), ("c4", 2), ("c3", 1),
+    ("c3", 3), ("t2", 4), ("g0", 0), ("d2", 3), ("t2", 5), ("c2", 4), ("c2", 5), ("c4", 1),
+    ("w", 1), ("w", 2), ("d1", 4), ("g1", 1), ("d1", 5), ("d3", 3), ("c4", 3), ("c3", 4),
+    ("g0", 1), ("d2", 4), ("c3", 5), ("g0", 2), ("d2", 5), ("w", 3), ("g1", 2), ("c4", 4),
+    ("d3", 4), ("g1", 3), ("d3", 5), ("g0", 3), ("c4", 5), ("w", 4), ("g0", 4), ("w", 5),
+    ("g0", 5), ("g1", 4), ("g1", 5),
 ]
 
 COPIES = [

time: 124 us -> 126 us (1.016)
    pallas_call x1, Pallas kernels: 120 us -> 121 us  [update(): pl.pallas_call(kernel, out_shape=pltpu.VMEM((height, width), BF16), in_sp...]
where the time goes in v6:
time: 126 us; the launch traced here: 125 us
  Pallas kernels  121 us (96%)
  local copies, waits for them, and re-layouts  3.74 us (3%)
    pallas_call x1, Pallas kernels, update(): pl.pallas_call(kernel, out_shape=pltpu.VMEM((height, width), BF16), in_sp...  121 us
    unnamed x1, local copies, waits for them, and re-layouts  3.74 us

profile of v6, /device:TPU:1, one launch (start us, length us, event | category | flops | bytes accessed | tf_op | source)
XLA Modules:
  0.0 125.1 jit_solution(6633480241588444940)
XLA Ops:
  0.0 121.4 %shard_map.46 = bf16[3072,1536]{1,0:T(8,128)(2,1)S(1)} custom-call(bf16[3072,1536]{1,0:T(8,128)(2,1)} %t_hbm.1, bf16[192,1280]{1,0:T(8,128)(2,1)} %b_own.1, s32[192,128]{1,0:T(8,128)} %bitcast.2, s32[192,128]{1,0:T(8,128)} %bitcast.3), custom_call_target="tpu_custom_call" | custom-call | flops 24159191040 | bytes 18874368 | tf_op jit(solution)/shard_map/pallas_call | solution.py:364
  121.4 3.7 %copy.6 = bf16[3072,1536]{1,0:T(8,128)(2,1)} copy(bf16[3072,1536]{1,0:T(8,128)(2,1)S(1)} %shard_map.46) | data formatting | bytes 18874368
